TPU v7x, 512 devices: a whole 4x4x16 slice. The times are simulated.
512 devices in a mesh: section: 16 (over y, z_hi, core), expert: 32 (over z_lo, x).
Axes of the slice: x: 4, y: 4, z: 16 (z_hi: 2, z_lo: 8; z = z_hi * 8 + z_lo), core: 2. Of those that a mesh axis runs over, the one named last changes fastest.
Arguments:
- cotangent: bfloat16 [16, 2, 2048, 3584], P('section', None, 'expert'), may hold values from -6 to 6
- routes: int32 [16, 2, 2048, 1], P('section', None, 'expert'), may hold values from 0 to 3; in each aligned block of 64 rows (0 to 63, 64 to 127, ..., all dimensions but the last counted through in order) at most 17 rows name the same one
- gate_prob: float32 [16, 2, 2048, 1], P('section', None, 'expert'), may hold values from 0.5 to 1.5
- saved_gate: bfloat16 [16, 2, 32, 17, 4096], P('section', None, None, None, 'expert'), may hold values from -6 to 6
- saved_up: bfloat16 [16, 2, 32, 17, 4096], P('section', None, None, None, 'expert'), may hold values from -6 to 6
- w_gate: bfloat16 [16, 3584, 4096], P('section', None, 'expert'), may hold values from -0.1875 to 0.1875
- w_up: bfloat16 [16, 3584, 4096], P('section', None, 'expert'), may hold values from -0.1875 to 0.1875
- w_down: bfloat16 [16, 4096, 3584], P('section', 'expert'), may hold values from -0.09375 to 0.09375
Outputs:
- input_grads: bfloat16 [16, 2, 2048, 3584], P('section', None, 'expert')
- gate_grads: float32 [16, 2, 2048, 1], P('section', None, 'expert')
Inputs may be any that keep to these rules, and one draw needn't show every extreme that they name: `routes`: among one index's 64 tokens of one micro-batch at most 17 choose the same expert.
All inputs are finite; a program needn't handle non-finite values.
Results may differ from a plain program's by a relative error of at most 0.01.
Values may be sent and summed in bfloat16 or wider, within the bound.
A program may use at most 128 MiB of HBM per device.

v0:
```python
import jax
import jax.numpy as jnp
from jax import lax
from jax.sharding import PartitionSpec as P

EXPERTS = 4


def passed_along(value, axis, steps):
    count = lax.axis_size(axis)
    leading, last = (max(0, -steps), min(count, count - steps))
    return lax.ppermute(value, axis, [(source, source + steps) for source in range(leading, last)])


def slot_layout(expert_ids, capacity):
    onehot = (expert_ids[:, None] == jnp.arange(EXPERTS, dtype=jnp.int32)[None, :]).astype(
        jnp.int32
    )
    slot_rank = jnp.sum((jnp.cumsum(onehot, axis=0) - 1) * onehot, axis=1)
    position = expert_ids * capacity + slot_rank
    return (position[:, None] == jnp.arange(EXPERTS * capacity, dtype=jnp.int32)[None, :]).astype(
        jnp.bfloat16
    )


def build_outgoing(incoming, slot_table, group_size):
    capacity = slot_table.shape[1] // EXPERTS
    width = incoming.shape[1]
    packed = lax.dot_general(
        slot_table, incoming, (((0,), (0,)), ((), ())), preferred_element_type=jnp.float32
    ).astype(jnp.bfloat16)
    packed = packed.reshape(EXPERTS, 1, capacity, width)
    return jnp.broadcast_to(packed, (EXPERTS, group_size, capacity, width)).reshape(
        EXPERTS * group_size, capacity, width
    )


def expert_backward(routed_rows, pre_gate, pre_up, weight_down, weight_both):
    sources = routed_rows.shape[0]
    slots = routed_rows.shape[1]
    flat_rows = routed_rows.reshape(sources * slots, routed_rows.shape[2])
    grad_hidden = lax.dot_general(
        flat_rows, weight_down, (((1,), (1,)), ((), ())), preferred_element_type=jnp.float32
    )
    gate_val = pre_gate.reshape(sources * slots, pre_gate.shape[2]).astype(jnp.float32)
    up_val = pre_up.reshape(sources * slots, pre_up.shape[2]).astype(jnp.float32)
    sigmoid_gate = 1.0 / (1.0 + jnp.exp(-gate_val))
    silu_gate = gate_val * sigmoid_gate
    score_part = jnp.sum(silu_gate * up_val * grad_hidden, axis=1).astype(jnp.bfloat16)
    grad_up = grad_hidden * silu_gate
    grad_gate = grad_hidden * up_val * sigmoid_gate * (1.0 + gate_val * (1.0 - sigmoid_gate))
    joined = jnp.concatenate([grad_gate.astype(jnp.bfloat16), grad_up.astype(jnp.bfloat16)], axis=1)
    partials = lax.dot_general(
        joined, weight_both, (((1,), (1,)), ((), ())), preferred_element_type=jnp.float32
    ).astype(jnp.bfloat16)
    return (partials.reshape(sources, slots, partials.shape[1]), score_part.reshape(sources, slots))


def combine_back(partials, score_part, slot_table, incoming, prob, group_size):
    capacity = partials.shape[1]
    table_three = slot_table.reshape(slot_table.shape[0], EXPERTS, capacity)
    grouped = partials.reshape(EXPERTS, group_size, capacity, partials.shape[2])
    summed = jnp.einsum("tec,egcd->td", table_three, grouped, preferred_element_type=jnp.float32)
    score_sum = jnp.einsum(
        "tec,egc->t",
        table_three,
        score_part.reshape(EXPERTS, group_size, capacity),
        preferred_element_type=jnp.float32,
    )
    result = (incoming.astype(jnp.float32) + prob * summed).astype(jnp.bfloat16)
    return (result, score_sum[:, None])


def on_device(cotangent, routes, gate_prob, saved_gate, saved_up, w_gate, w_up, w_down):
    devices = lax.axis_size("expert")
    group_size = devices // EXPERTS
    capacity = saved_gate.shape[3]
    micros = cotangent.shape[1]
    weight_both = jnp.concatenate([w_gate[0], w_up[0]], axis=1)
    weight_down = w_down[0]
    tables = [slot_layout(routes[0, microbatch, :, 0], capacity) for microbatch in range(micros)]
    outgoing = [
        build_outgoing(cotangent[0, microbatch], tables[microbatch], group_size)
        for microbatch in range(micros)
    ]
    results = []
    for microbatch in range(micros):
        arrived = lax.all_to_all(
            outgoing[microbatch], "expert", split_axis=0, concat_axis=0, tiled=True
        )
        partials, score_part = expert_backward(
            arrived, saved_gate[0, microbatch], saved_up[0, microbatch], weight_down, weight_both
        )
        partials, score_part = (
            lax.all_to_all(partials, "expert", split_axis=0, concat_axis=0, tiled=True),
            lax.all_to_all(score_part, "expert", split_axis=0, concat_axis=0, tiled=True),
        )
        results.append(
            combine_back(
                partials,
                score_part,
                tables[microbatch],
                cotangent[0, microbatch],
                gate_prob[0, microbatch],
                group_size,
            )
        )
    handed = passed_along(results[0][0], "section", -1)
    grads_out = jnp.stack([handed] + [outcome[0] for outcome in results[1:]], axis=0)[None]
    scores_out = jnp.stack([outcome[1] for outcome in results], axis=0)[None]
    return (grads_out, scores_out)


def solution(mesh):
    in_specs = (
        P("section", None, "expert", None),
        P("section", None, "expert", None),
        P("section", None, "expert", None),
        P("section", None, None, None, "expert"),
        P("section", None, None, None, "expert"),
        P("section", None, "expert"),
        P("section", None, "expert"),
        P("section", "expert", None),
    )
    out_specs = (P("section", None, "expert", None), P("section", None, "expert", None))
    return jax.shard_map(
        on_device, mesh=mesh, in_specs=in_specs, out_specs=out_specs, check_vma=False
    )
```

profile of v0, /device:TPU:24, one launch (start us, length us, event | category | flops | bytes accessed | tf_op | source)
XLA Modules:
  0.0 1091.6 jit_solution(588548499347876303)
XLA Ops:
  0.6 0.8 slice_bitcast_fusion.2
  1.6 0.1 reduce_window_sum.17
  1.6 0.1 reduce_window_sum.18
  1.7 0.2 select_reduce_fusion
  1.9 0.7 multiply_add_fusion.2
  2.6 1.4 convolution_convert_fusion.3
  4.0 0.2 broadcast_in_dim.12
  4.2 2.8 broadcast_in_dim.13
  7.0 15.6 %all-to-all-start = ((bf16[32,17,3584]{2,1,0:T(8,128)(2,1)}), bf16[32,17,3584]{2,1,0:T(8,128)(2,1)}, u32[]{:S(2)}, u32[]{:S(2)}) async-start(bf16[32,17,3584]{2,1,0:T(8,128)(2,1)} %bitcast.93), calls=%async_computation | async-start | bytes 11010048 | tf_op jit(solution)/shard_map/all_to_all | solution.py:88
  22.6 0.4 convolution_convert_fusion.2
  23.0 0.2 broadcast_in_dim.28
  23.2 244.8 %all-to-all-done = bf16[32,17,3584]{2,1,0:T(8,128)(2,1)} async-done(((bf16[32,17,3584]{2,1,0:T(8,128)(2,1)}), bf16[32,17,3584]{2,1,0:T(8,128)(2,1)}, u32[]{:S(2)}, u32[]{:S(2)}) %all-to-all-start) | async-done | bytes 3899424 | tf_op jit(solution)/shard_map/all_to_all | solution.py:88
  268.0 2.8 broadcast_in_dim.29
  270.9 5.5 all-to-all-start.2
  276.5 0.2 copy.20
  276.7 0.7 reshape.128
  277.4 0.2 copy.21
  277.6 0.7 reshape.129
  278.3 0.2 copy.22
  278.5 0.2 copy.23
  278.8 5.6 reshape.123
  284.4 3.9 multiply_reduce_fusion.1
  288.3 0.7 convert_element_type.168
  289.1 233.8 %all-to-all-done.2 = bf16[32,17,3584]{2,1,0:T(8,128)(2,1)} async-done(((bf16[32,17,3584]{2,1,0:T(8,128)(2,1)}), bf16[32,17,3584]{2,1,0:T(8,128)(2,1)}, u32[]{:S(2)}, u32[]{:S(2)}) %all-to-all-start.2) | async-done | bytes 3899424 | tf_op jit(solution)/shard_map/all_to_all | solution.py:88
  522.9 4.1 all-to-all-start.4
  527.0 5.6 reshape.126
  532.6 4.1 multiply_reduce_fusion
  536.7 0.7 convert_element_type.169
  537.4 2.2 all-to-all-done.4
  539.6 10.4 all-to-all-start.5
  549.9 4.4 convolution_convert_fusion.1
  554.3 5.5 reshape.124
  559.9 2.6 all-to-all-done.5
  562.5 10.2 all-to-all-start.1
  572.7 3.1 convolution_convert_fusion
  575.8 5.6 reshape.127
  581.4 232.7 %all-to-all-done.1 = bf16[32,17,3584]{2,1,0:T(8,128)(2,1)} async-done(((bf16[32,17,3584]{2,1,0:T(8,128)(2,1)}), bf16[32,17,3584]{2,1,0:T(8,128)(2,1)}, u32[]{:S(2)}, u32[]{:S(2)}) %all-to-all-start.1) | async-done | bytes 3899424 | tf_op jit(solution)/shard_map/all_to_all | solution.py:95
  814.1 7.9 all-to-all-start.3
  822.1 0.2 convolution_bitcast_fusion.3
  822.3 0.2 convolution_bitcast_fusion.2
  822.5 0.6 maximum_bitcast_fusion.1
  823.1 3.4 convert_reduce_fusion.1
  826.5 0.4 fusion.4
  826.9 7.5 collective-permute-start
  834.4 252.3 %all-to-all-done.3 = bf16[32,17,3584]{2,1,0:T(8,128)(2,1)} async-done(((bf16[32,17,3584]{2,1,0:T(8,128)(2,1)}), bf16[32,17,3584]{2,1,0:T(8,128)(2,1)}, u32[]{:S(2)}, u32[]{:S(2)}) %all-to-all-start.3) | async-done | bytes 3899424 | tf_op jit(solution)/shard_map/all_to_all | solution.py:95
  1086.8 3.4 convert_reduce_fusion
  1090.2 0.4 fusion.6
  1090.6 1.0 maximum_bitcast_fusion
  (37 shorter events, 0.4 us)
Async XLA Ops:
  0.6 283.8 %copy-start = (bf16[1,128,3584]{2,1,0:T(8,128)(2,1)S(1)}, bf16[1,128,3584]{2,1,0:T(8,128)(2,1)}, u32[]{:S(2)}) copy-start(bf16[1,128,3584]{2,1,0:T(8,128)(2,1)} %param.15) | copy-start | bytes 2752516
  7.0 15.6 %copy-start.2 = (bf16[1,2,64,3584]{3,2,1,0:T(8,128)(2,1)S(1)}, bf16[1,2,64,3584]{3,2,1,0:T(8,128)(2,1)}, u32[]{:S(2)}) copy-start(bf16[1,2,64,3584]{3,2,1,0:T(8,128)(2,1)} %param.8) | copy-start | bytes 2752516
  7.0 261.1 %all-to-all-start = ((bf16[32,17,3584]{2,1,0:T(8,128)(2,1)}), bf16[32,17,3584]{2,1,0:T(8,128)(2,1)}, u32[]{:S(2)}, u32[]{:S(2)}) async-start(bf16[32,17,3584]{2,1,0:T(8,128)(2,1)} %bitcast.93), calls=%async_computation | async-start | bytes 11010048 | tf_op jit(solution)/shard_map/all_to_all | solution.py:88
  270.9 5.5 copy-start.5
  270.9 6.5 copy-start.6
  270.9 252.0 %all-to-all-start.2 = ((bf16[32,17,3584]{2,1,0:T(8,128)(2,1)}), bf16[32,17,3584]{2,1,0:T(8,128)(2,1)}, u32[]{:S(2)}, u32[]{:S(2)}) async-start(bf16[32,17,3584]{2,1,0:T(8,128)(2,1)} %bitcast.92), calls=%async_computation.2 | async-start | bytes 11010048 | tf_op jit(solution)/shard_map/all_to_all | solution.py:88
  278.8 5.6 copy-start.7
  278.8 5.6 copy-start.8
  522.9 16.7 %all-to-all-start.4 = ((bf16[32,1,17]{2,1,0:T(2,128)(2,1)}), bf16[32,1,17]{2,1,0:T(2,128)(2,1)S(1)}, u32[]{:S(2)}, u32[]{:S(2)}) async-start(bf16[32,1,17]{2,1,0:T(2,128)(2,1)} %convert_element_type.168), calls=%async_computation.4 | async-start | bytes 32768 | tf_op jit(solution)/shard_map/all_to_all | solution.py:96
  532.6 17.3 %copy-start.3 = (bf16[1,3584,128]{2,1,0:T(8,128)(2,1)S(1)}, bf16[1,3584,128]{2,1,0:T(8,128)(2,1)}, u32[]{:S(2)}) copy-start(bf16[1,3584,128]{2,1,0:T(8,128)(2,1)} %param.14) | copy-start | bytes 2752516
  539.6 22.9 %all-to-all-start.5 = ((bf16[32,1,17]{2,1,0:T(2,128)(2,1)}), bf16[32,1,17]{2,1,0:T(2,128)(2,1)S(1)}, u32[]{:S(2)}, u32[]{:S(2)}) async-start(bf16[32,1,17]{2,1,0:T(2,128)(2,1)} %convert_element_type.169), calls=%async_computation.5 | async-start | bytes 32768 | tf_op jit(solution)/shard_map/all_to_all | solution.py:96
  559.9 12.8 %copy-start.4 = (bf16[1,3584,128]{2,1,0:T(8,128)(2,1)S(1)}, bf16[1,3584,128]{2,1,0:T(8,128)(2,1)}, u32[]{:S(2)}) copy-start(bf16[1,3584,128]{2,1,0:T(8,128)(2,1)} %param.13) | copy-start | bytes 2752516
  559.9 12.8 %copy-start.9 = (bf16[544,128]{1,0:T(8,128)(2,1)S(1)}, bf16[544,128]{1,0:T(8,128)(2,1)}, u32[]{:S(2)}) copy-start(bf16[544,128]{1,0:T(8,128)(2,1)} %get-tuple-element.11) | copy-start | bytes 417796
  559.9 12.8 %copy-start.10 = (bf16[544,128]{1,0:T(8,128)(2,1)S(1)}, bf16[544,128]{1,0:T(8,128)(2,1)}, u32[]{:S(2)}) copy-start(bf16[544,128]{1,0:T(8,128)(2,1)} %get-tuple-element.13) | copy-start | bytes 417796
  562.5 251.5 %all-to-all-start.1 = ((bf16[32,17,3584]{2,1,0:T(8,128)(2,1)}), bf16[32,17,3584]{2,1,0:T(8,128)(2,1)}, u32[]{:S(2)}, u32[]{:S(2)}) async-start(bf16[32,17,3584]{2,1,0:T(8,128)(2,1)} %reshape.124), calls=%async_computation.1 | async-start | bytes 11010048 | tf_op jit(solution)/shard_map/all_to_all | solution.py:95
  581.4 240.6 %copy-start.11 = (f32[1,2,64,1]{2,3,1,0:T(1,128)S(1)}, f32[1,2,64,1]{2,3,1,0:T(1,128)}, u32[]{:S(2)}) copy-start(f32[1,2,64,1]{2,3,1,0:T(1,128)} %param.10) | copy-start | bytes 1540
  814.1 272.7 %all-to-all-start.3 = ((bf16[32,17,3584]{2,1,0:T(8,128)(2,1)}), bf16[32,17,3584]{2,1,0:T(8,128)(2,1)}, u32[]{:S(2)}, u32[]{:S(2)}) async-start(bf16[32,17,3584]{2,1,0:T(8,128)(2,1)} %reshape.127), calls=%async_computation.3 | async-start | bytes 11010048 | tf_op jit(solution)/shard_map/all_to_all | solution.py:95
  826.5 265.1 %copy-start.1 = (bf16[1,128,3584]{2,1,0:T(8,128)(2,1)S(1)}, bf16[1,128,3584]{2,1,0:T(8,128)(2,1)}, u32[]{:S(2)}) copy-start(bf16[1,128,3584]{2,1,0:T(8,128)(2,1)} %param.15) | copy-start | bytes 2752516
  826.9 263.6 %collective-permute-start = (bf16[64,3584]{1,0:T(8,128)(2,1)S(1)}, bf16[64,3584]{1,0:T(8,128)(2,1)S(1)}, u32[]{:S(2)}, u32[]{:S(2)}) collective-permute-start(bf16[64,3584]{1,0:T(8,128)(2,1)S(1)} %fusion.4), channel_id=1, source_target_pairs={{32,0},{64,32},{96,64},{128,96},{160,128},{192,160},{224,192},{256... | collective-permute-start | bytes 1376264 | tf_op jit(solution)/shard_map/ppermute | solution.py:12
where the time goes:
time: 1090 us
  waiting for transfers between devices  968 us (89%)
  starting transfers between devices  61.2 us (6%)
  local copies, waits for them, and re-layouts  32.7 us (3%)
  matrix products  18.5 us (2%)
    all_to_all x2, waiting for transfers between devices, on_device(): lax.all_to_all(partials, 'expert', split_axis=0, concat_axis=0, tiled=True)  485 us
    all_to_all x2, waiting for transfers between devices, on_device(): lax.all_to_all(outgoing[microbatch], 'expert', split_axis=0, concat_axis=...  479 us
  transfers between devices with their start and end apart: 7, of which 6 were waited for; matrix products, arithmetic and copies ran while one was open for 5% of the time, Pallas kernels for 0%

commit v1 on v0

v1 whole, which is shorter than its diff:
```python
import jax
import jax.numpy as jnp
from jax import lax
from jax.experimental import pallas as pl
from jax.experimental.pallas import tpu as pltpu
from jax.sharding import PartitionSpec as P

MESH = pl.DeviceIdType.MESH
BF16 = jnp.bfloat16
F32 = jnp.float32

TOK = 64
D = 3584
X = 4
Z = 8
EXPERTS = 4
SLICE = D // X
CHUNKS = SLICE // 128
TILE = 16
WIDE = SLICE + 128
SOURCES = X * Z
MAIN = SOURCES * TILE
ROWS = MAIN + SOURCES
FH = 128
BAND = X * TILE
SCORE_ROW = 8


def dot(a, b):
    return lax.dot_general(a, b, (((1,), (0,)), ((), ())), preferred_element_type=F32)


def dot_t(a, b):
    return lax.dot_general(a, b, (((1,), (1,)), ((), ())), preferred_element_type=F32)


def iota(shape, axis):
    return lax.broadcasted_iota(jnp.int32, shape, axis)


def waited(ref, sem):
    pltpu.make_async_copy(ref, ref, sem).wait()


def kernel(
    ids_col, ids_row, prob, cot, saved_gate, saved_up, w_gate, w_up, w_down,
    out, scores,
    sent, routed, wd, wg, wu, a_sent, a_got, hidden, part, mate_part, total, back, handed,
    send_sem, routed_sem, relay_sem, w_send, w_sem, w_own, a_send, a_sem, h_send, h_sem,
    mate_send, mate_sem, total_send, back_sem, hand_send, hand_sem,
):
    sec = lax.axis_index("section")
    me = lax.axis_index("expert")
    sections = lax.axis_size("section")
    z, x = me // X, me % X
    expert, side = z // 2, z % 2
    mate = z + 1 - 2 * side
    mate_id = mate * X + x
    owned = jnp.where(side == 0, z + 1, Z - z)
    others = jnp.where(side == 0, Z - mate, mate + 1)
    away = jnp.where(side == 0, -1, 1)

    def at(index):
        return dict(device_id={"expert": index}, device_id_type=MESH)

    def band(plane):
        return pl.ds(pl.multiple_of(plane * BAND, BAND), BAND)

    def rows16(index):
        return pl.ds(pl.multiple_of(index * TILE, TILE), TILE)

    barrier = pltpu.get_barrier_semaphore()

    def greet(step, carry):
        pl.semaphore_signal(barrier, inc=1, **at((me + step) % (X * Z)))
        return carry

    lax.fori_loop(1, X * Z, greet, 0)

    @pl.when(sec > 0)
    def _():
        pl.semaphore_signal(barrier, inc=1, device_id={"section": sec - 1}, device_id_type=MESH)

    @pl.when(sec < sections - 1)
    def _():
        pl.semaphore_signal(barrier, inc=1, device_id={"section": sec + 1}, device_id_type=MESH)

    ends = jnp.where(sec > 0, 1, 0) + jnp.where(sec < sections - 1, 1, 0)

    def pack(mb):
        ids = ids_row[mb]
        hot = (iota((8, TOK), 0) == ids).astype(F32)
        before = (iota((TOK, TOK), 0) < iota((TOK, TOK), 1)).astype(BF16)
        rank = jnp.sum(dot(hot.astype(BF16), before) * hot, axis=0, keepdims=True).astype(jnp.int32)
        row = iota((2 * TOK, TOK), 0)
        main = jnp.logical_and(row == ids * TILE + rank, jnp.logical_and(rank < TILE, row < TOK))
        last = jnp.logical_and((row - TOK) // TILE == ids, jnp.logical_and(rank == TILE, row >= TOK))
        pick = jnp.logical_or(main, last).astype(BF16)
        place = iota((TOK, 128), 0) % TILE
        for d in range(X):
            picked = dot(pick, cot[mb, :, d * SLICE : (d + 1) * SLICE])
            sent[mb, d, :, 0:SLICE] = picked[0:TOK].astype(BF16)
            folded = jnp.zeros((TOK, 128), F32)
            for k in range(CHUNKS):
                folded = jnp.where(place == k, picked[TOK:, k * 128 : (k + 1) * 128], folded)
            sent[mb, d, :, SLICE:WIDE] = folded.astype(BF16)

    def dispatch(mb):
        def one(step, carry):
            far = step // X
            e = jnp.where(z < Z // 2, EXPERTS - 1 - far, far)
            d = (x + 1 + step) % X
            near = jnp.where(z <= 2 * e, 2 * e, 2 * e + 1)
            target = near * X + d
            src = sent.at[mb, d, rows16(e), :]
            dst = routed.at[mb, rows16(me), :]

            @pl.when(target == me)
            def _():
                pltpu.make_async_copy(src, dst, routed_sem.at[mb, z]).start()

            @pl.when(target != me)
            def _():
                pltpu.make_async_remote_copy(
                    src, dst, send_sem.at[mb], routed_sem.at[mb, z], **at(target)
                ).start()

            return carry

        lax.fori_loop(0, X * EXPERTS, one, 0)

    def relay(mb, first, last):
        def one(step, carry):
            plane = z + away * step
            block = routed.at[mb, band(plane), :]
            waited(block, routed_sem.at[mb, plane])
            pltpu.make_async_remote_copy(
                block, block, relay_sem.at[mb, plane], routed_sem.at[mb, plane], **at(mate_id)
            ).start()
            return carry

        lax.fori_loop(first, last, one, 0)

    def arrivals(mb):
        def one(step, carry):
            plane = mate - away * step
            waited(routed.at[mb, band(plane), :], routed_sem.at[mb, plane])
            return carry

        lax.fori_loop(0, others, one, 0)

    def weights():
        for j in range(X):
            d = (x + j) % X
            across = pl.ds(pl.multiple_of(d * SLICE, 128), SLICE)
            pairs = (
                (w_down.at[:, across], wd.at[j]),
                (w_gate.at[across, :], wg.at[j]),
                (w_up.at[across, :], wu.at[j]),
            )
            for which, (src, dst) in enumerate(pairs):
                if j == 0:
                    pltpu.make_async_copy(src, dst, w_own.at[which]).start()
                else:
                    pltpu.make_async_remote_copy(
                        src, dst, w_send.at[which, j - 1], w_sem.at[which, j - 1], **at(z * X + d)
                    ).start()

    def weights_here(which, ref):
        waited(ref.at[0], w_own.at[which])
        for j in range(1, X):
            waited(ref.at[j], w_sem.at[which, j - 1])

    def first_product(mb):
        row = iota((CHUNKS * SOURCES, MAIN), 0)
        unfold = (iota((CHUNKS * SOURCES, MAIN), 1) == (row % SOURCES) * TILE + row // SOURCES).astype(BF16)
        tail = dot(unfold, routed[mb, :, SLICE:WIDE]).astype(BF16)
        tail = jnp.concatenate(
            [tail[k * SOURCES : (k + 1) * SOURCES] for k in range(CHUNKS)], axis=1
        )
        for j in range(X):
            a_sent[mb, j, 0:MAIN] = dot_t(routed[mb, :, 0:SLICE], wd[j]).astype(BF16)
            a_sent[mb, j, MAIN:ROWS] = dot_t(tail, wd[j]).astype(BF16)
        for j in range(1, X):
            pltpu.make_async_remote_copy(
                a_sent.at[mb, j], a_got.at[mb, j - 1], a_send.at[mb, j - 1], a_sem.at[mb, j - 1],
                **at(z * X + (x + X - j) % X),
            ).start()

    def activate(mb):
        for j in range(1, X):
            waited(a_got.at[mb, j - 1], a_sem.at[mb, j - 1])
        a = a_sent[mb, 0].astype(F32)
        for j in range(1, X):
            a = a + a_got[mb, j - 1].astype(F32)
        g = saved_gate[mb].astype(F32)
        u = saved_up[mb].astype(F32)
        sg = 1.0 / (1.0 + jnp.exp(-g))
        grad_up = a * (g * sg)
        grad_gate = a * u * sg * (1.0 + g * (1.0 - sg))
        hidden[mb, 0, :, 0:FH] = grad_gate.astype(BF16)
        hidden[mb, 0, :, FH : 2 * FH] = grad_up.astype(BF16)
        for j in range(1, X):
            pltpu.make_async_remote_copy(
                hidden.at[mb, 0], hidden.at[mb, j], h_send.at[mb, j - 1], h_sem.at[mb, j - 1],
                **at(z * X + (x + j) % X),
            ).start()
        score = jnp.sum(grad_up * u, axis=1, keepdims=True)
        row = iota((ROWS, 128), 0)
        slot = jnp.where(row < MAIN, row % TILE, TILE)
        spread = jnp.where(iota((ROWS, 128), 1) == slot, score, 0.0).astype(BF16)
        row, other = iota((MAIN, ROWS), 0), iota((MAIN, ROWS), 1)
        source = jnp.where(other < MAIN, other // TILE, other - MAIN)
        gather = jnp.logical_and(row % TILE == SCORE_ROW, row // TILE == source).astype(BF16)
        part[mb, :, SLICE:WIDE] = dot(gather, spread).astype(BF16)

    def second_product(mb):
        for j in range(1, X):
            waited(hidden.at[mb, j], h_sem.at[mb, j - 1])
        grads = jnp.zeros((ROWS, SLICE), F32)
        for j in range(X):
            both = jnp.concatenate([wg[j], wu[j]], axis=1)
            grads = grads + dot_t(hidden[mb, j], both)
        part[mb, :, 0:SLICE] = grads[0:MAIN].astype(BF16)
        tail = grads[MAIN:ROWS].astype(BF16)
        spread = dot((iota((MAIN, SOURCES), 0) // TILE == iota((MAIN, SOURCES), 1)).astype(BF16), tail)
        place = iota((MAIN, 128), 0) % TILE
        folded = part[mb, :, SLICE:WIDE].astype(F32)
        for k in range(CHUNKS):
            folded = jnp.where(place == k, spread[:, k * 128 : (k + 1) * 128], folded)
        part[mb, :, SLICE:WIDE] = folded.astype(BF16)

        def one(step, carry):
            plane = mate - away * step
            pltpu.make_async_remote_copy(
                part.at[mb, band(plane), :], mate_part.at[mb, band(plane), :],
                mate_send.at[mb, plane], mate_sem.at[mb, plane], **at(mate_id),
            ).start()
            return carry

        lax.fori_loop(0, others, one, 0)

    def send_back(mb):
        def one(step, carry):
            plane = z + away * (owned - 1 - step)
            rows = band(plane)
            waited(mate_part.at[mb, rows, :], mate_sem.at[mb, plane])
            both = part[mb, rows, :].astype(F32) + mate_part[mb, rows, :].astype(F32)
            total[mb, rows, :] = both.astype(BF16)

            def to(step, carry):
                target = plane * X + (x + 1 + step) % X
                src = total.at[mb, rows16(target), :]
                dst = back.at[mb, x, rows16(expert), :]

                @pl.when(target == me)
                def _():
                    pltpu.make_async_copy(src, dst, back_sem.at[mb]).start()

                @pl.when(target != me)
                def _():
                    pltpu.make_async_remote_copy(
                        src, dst, total_send.at[mb, plane], back_sem.at[mb], **at(target)
                    ).start()

                return carry

            lax.fori_loop(0, X, to, 0)
            return carry

        lax.fori_loop(0, owned, one, 0)

    def finish(mb):
        waited(back.at[mb], back_sem.at[mb])
        ids = ids_col[mb]
        lane = iota((TOK, 128), 1)
        hot = (lane == ids).astype(F32)
        before = (iota((TOK, TOK), 1) < iota((TOK, TOK), 0)).astype(BF16)
        rank = jnp.sum(dot(before, hot.astype(BF16)) * hot, axis=1, keepdims=True).astype(jnp.int32)
        column = iota((TOK, TOK), 1)
        main = jnp.logical_and(column == ids * TILE + rank, rank < TILE).astype(BF16)
        group = [
            jnp.logical_and(column == ids * TILE + k, rank == TILE).astype(F32) for k in range(CHUNKS)
        ]
        group.append((column == ids * TILE + SCORE_ROW).astype(F32))
        pick = jnp.concatenate(group, axis=0).astype(BF16)
        score = jnp.zeros((TOK, 128), F32)
        weight = prob[mb]
        for d in range(X):
            tail = dot(pick, back[mb, d, :, SLICE:WIDE])
            score = score + tail[CHUNKS * TOK :]
            grads = dot(main, back[mb, d, :, 0:SLICE])
            grads = grads + jnp.concatenate(
                [tail[k * TOK : (k + 1) * TOK] for k in range(CHUNKS)], axis=1
            )
            across = slice(d * SLICE, (d + 1) * SLICE)
            dx = (cot[mb, :, across].astype(F32) + weight * grads).astype(BF16)
            if mb == 0:
                handed[:, across] = dx
            else:
                out[mb, :, across] = dx
        scores[mb] = jnp.sum(jnp.where(lane == rank, score, 0.0), axis=1, keepdims=True)

    pack(0)
    pl.semaphore_wait(barrier, X * Z - 1 + ends)
    dispatch(0)
    weights()
    pack(1)
    dispatch(1)
    relay(0, 0, owned)
    arrivals(0)
    weights_here(0, wd)
    first_product(0)
    half = (owned + 1) // 2
    relay(1, 0, half)
    activate(0)
    relay(1, half, owned)
    arrivals(1)
    first_product(1)
    weights_here(1, wg)
    weights_here(2, wu)
    second_product(0)
    activate(1)
    send_back(0)
    second_product(1)
    send_back(1)
    finish(0)

    @pl.when(sec > 0)
    def _():
        pltpu.make_async_remote_copy(
            handed, out.at[0], hand_send, hand_sem, device_id={"section": sec - 1}, device_id_type=MESH
        ).start()

    @pl.when(sec == sections - 1)
    def _():
        out[0] = jnp.zeros((TOK, D), BF16)

    finish(1)

    for mb in range(2):
        waited(routed.at[mb, pl.ds(0, (X * EXPERTS - 1) * TILE), :], send_sem.at[mb])

        def relayed(step, carry):
            plane = z + away * step
            waited(routed.at[mb, band(plane), :], relay_sem.at[mb, plane])
            rows = total.at[mb, band(plane), :]

            @pl.when(plane == z)
            def _():
                waited(total.at[mb, pl.ds(0, BAND - TILE), :], total_send.at[mb, plane])

            @pl.when(plane != z)
            def _():
                waited(rows, total_send.at[mb, plane])

            return carry

        lax.fori_loop(0, owned, relayed, 0)

        def mated(step, carry):
            plane = mate - away * step
            waited(part.at[mb, band(plane), :], mate_send.at[mb, plane])
            return carry

        lax.fori_loop(0, others, mated, 0)
        for j in range(1, X):
            waited(a_sent.at[mb, j], a_send.at[mb, j - 1])
            waited(hidden.at[mb, 0], h_send.at[mb, j - 1])
    for which, ref in enumerate((wd, wg, wu)):
        for j in range(1, X):
            waited(ref.at[j], w_send.at[which, j - 1])

    @pl.when(sec > 0)
    def _():
        waited(handed, hand_send)

    @pl.when(sec < sections - 1)
    def _():
        waited(out.at[0], hand_sem)


def on_device(cotangent, routes, gate_prob, saved_gate, saved_up, w_gate, w_up, w_down):
    def by_row(saved):
        main = saved[0, :, :, :TILE, :].reshape(2, MAIN, FH)
        return jnp.concatenate([main, saved[0, :, :, TILE, :]], axis=1)

    vmem = pl.BlockSpec(memory_space=pltpu.VMEM)
    hbm = pl.BlockSpec(memory_space=pl.ANY)
    dma = pltpu.SemaphoreType.DMA
    grads, scores = pl.pallas_call(
        kernel,
        out_shape=(
            jax.ShapeDtypeStruct((2, TOK, D), BF16),
            jax.ShapeDtypeStruct((2, TOK, 1), F32),
        ),
        in_specs=[vmem] * 6 + [hbm] * 3,
        out_specs=(vmem, vmem),
        scratch_shapes=[
            pltpu.VMEM((2, X, TOK, WIDE), BF16),
            pltpu.VMEM((2, MAIN, WIDE), BF16),
            pltpu.VMEM((X, FH, SLICE), BF16),
            pltpu.VMEM((X, SLICE, FH), BF16),
            pltpu.VMEM((X, SLICE, FH), BF16),
            pltpu.VMEM((2, X, ROWS, FH), BF16),
            pltpu.VMEM((2, X - 1, ROWS, FH), BF16),
            pltpu.VMEM((2, X, ROWS, 2 * FH), BF16),
            pltpu.VMEM((2, MAIN, WIDE), BF16),
            pltpu.VMEM((2, MAIN, WIDE), BF16),
            pltpu.VMEM((2, MAIN, WIDE), BF16),
            pltpu.VMEM((2, X, TOK, WIDE), BF16),
            pltpu.VMEM((TOK, D), BF16),
            dma((2,)),
            dma((2, Z)),
            dma((2, Z)),
            dma((3, X - 1)),
            dma((3, X - 1)),
            dma((3,)),
            dma((2, X - 1)),
            dma((2, X - 1)),
            dma((2, X - 1)),
            dma((2, X - 1)),
            dma((2, Z)),
            dma((2, Z)),
            dma((2, Z)),
            dma((2,)),
            dma,
            dma,
        ],
        compiler_params=pltpu.CompilerParams(
            collective_id=0, has_side_effects=True, vmem_limit_bytes=48 * 1024 * 1024
        ),
        cost_estimate=pl.CostEstimate(
            flops=6 * 2 * ROWS * D * FH, bytes_accessed=8 * 1024 * 1024, transcendentals=2 * ROWS * FH
        ),
    )(
        routes[0],
        routes[0].reshape(2, 1, TOK),
        gate_prob[0],
        cotangent[0],
        by_row(saved_gate),
        by_row(saved_up),
        w_gate[0],
        w_up[0],
        w_down[0],
    )
    return grads[None], scores[None]


def solution(mesh):
    in_specs = (
        P("section", None, "expert", None),
        P("section", None, "expert", None),
        P("section", None, "expert", None),
        P("section", None, None, None, "expert"),
        P("section", None, None, None, "expert"),
        P("section", None, "expert"),
        P("section", None, "expert"),
        P("section", "expert", None),
    )
    out_specs = (P("section", None, "expert", None), P("section", None, "expert", None))
    return jax.shard_map(
        on_device, mesh=mesh, in_specs=in_specs, out_specs=out_specs, check_vma=False
    )
```

time: 1090 us -> 199 us (0.18)
  the two profiles are of different devices: /device:TPU:24 before, /device:TPU:112 now
where the time goes in v1:
time: 199 us
  Pallas kernels  190 us (95%)
  local copies, waits for them, and re-layouts  7.37 us (4%)
    pallas_call x1, Pallas kernels, on_device(): pl.pallas_call(kernel, out_shape=(jax.ShapeDtypeStruct((2, TOK, D), BF16)...  190 us

profile of v1, /device:TPU:112, one launch (start us, length us, event | category | flops | bytes accessed | tf_op | source)
XLA Modules:
  0.0 199.0 jit_solution(1882583673587273788)
XLA Ops:
  0.6 0.7 slice_bitcast_fusion.1
  1.4 0.0 copy-start.5
  1.4 0.7 slice_bitcast_fusion
  2.1 0.0 copy-done.5
  2.1 0.0 copy-start
  2.1 0.1 copy.24.prob
  2.2 0.6 copy-done
  2.8 0.0 slice-start
  2.8 0.1 copy.22.ids_col
  2.9 0.0 copy-start.3
  2.9 0.8 slice-done
  3.7 0.0 slice-start.1
  3.7 0.1 copy.18
  3.8 0.0 copy-start.2
  3.8 0.9 slice-done.1
  4.7 0.0 copy-start.1
  4.7 0.1 copy.20
  4.9 0.0 copy-done.3
  4.9 0.2 copy-done.2
  5.1 0.9 copy-done.1
  6.0 0.0 copy-start.4
  6.0 1.2 copy-done.4
  7.2 190.2 %shard_map.95 = (bf16[2,64,3584]{2,1,0:T(8,128)(2,1)S(1)}, f32[2,64,1]{2,1,0:T(8,128)S(1)}) custom-call(s32[2,64,1]{2,1,0:T(8,128)S(1)} %copy.22.ids_col, s32[2,1,64]{2,1,0:T(1,128)S(1)} %bitcast.25, f32[2,64,1]{2,1,0:T(8,128)S(1)} %copy.24.prob, bf16[2,64,3584]{2,1,0:T(8,128)(2,1)S(1)} %bitcast.26, bf16[2,544,128]{2,1,0:T(8,128)(2,1)S(1)} %get-tuple-element.10.saved_gate, ...), custom_call_target="tpu_custom_call" | custom-call | flops 2994733056 | bytes 8388608 | tf_op jit(solution)/shard_map/pallas_call | solution.py:391
  197.4 0.7 reduce
  198.1 0.9 copy.29
  (1 shorter events, 0.0 us)
Async XLA Ops:
  1.4 0.7 copy-start.5
  2.1 0.7 copy-start
  2.8 0.9 slice-start
  2.9 2.0 %copy-start.3 = (bf16[1,3584,128]{2,1,0:T(8,128)(2,1)S(1)}, bf16[1,3584,128]{2,1,0:T(8,128)(2,1)}, u32[]{:S(2)}) copy-start(bf16[1,3584,128]{2,1,0:T(8,128)(2,1)} %param.14) | copy-start | bytes 2752516
  3.7 1.0 slice-start.1
  3.8 1.3 copy-start.2
  4.7 1.2 copy-start.1
  6.0 1.2 copy-start.4

commit v2 on v1

--- a/solution.py
+++ b/solution.py
@@ -23,6 +23,7 @@
 ROWS = MAIN + SOURCES
 FH = 128
 BAND = X * TILE
+VMEM_MB = 28
 SCORE_ROW = 8
 
 
@@ -43,9 +44,10 @@
 
 
 def kernel(
-    ids_col, ids_row, prob, cot, saved_gate, saved_up, w_gate, w_up, w_down,
+    ids_col, ids_row, prob, cot_hbm, gate_hbm, up_hbm, w_gate, w_up, w_down,
     out, scores,
-    sent, routed, wd, wg, wu, a_sent, a_got, hidden, part, mate_part, total, back, handed,
+    cot, saved_gate, saved_up, in_sem,
+    sent0, sent1, routed0, routed1, wd, wg, wu, a_sent, a_got, hidden, part, mate_part, total, back, handed,
     send_sem, routed_sem, relay_sem, w_send, w_sem, w_own, a_send, a_sem, h_send, h_sem,
     mate_send, mate_sem, total_send, back_sem, hand_send, hand_sem,
 ):
@@ -69,6 +71,13 @@
     def rows16(index):
         return pl.ds(pl.multiple_of(index * TILE, TILE), TILE)
 
+    sent, routed = (sent0, sent1), (routed0, routed1)
+    loads = [
+        pltpu.make_async_copy(src, dst, in_sem.at[which])
+        for which, (src, dst) in enumerate(((cot_hbm, cot), (gate_hbm, saved_gate), (up_hbm, saved_up)))
+    ]
+    for load in loads:
+        load.start()
     barrier = pltpu.get_barrier_semaphore()
 
     def greet(step, carry):
@@ -87,23 +96,27 @@
 
     ends = jnp.where(sec > 0, 1, 0) + jnp.where(sec < sections - 1, 1, 0)
 
-    def pack(mb):
-        ids = ids_row[mb]
-        hot = (iota((8, TOK), 0) == ids).astype(F32)
-        before = (iota((TOK, TOK), 0) < iota((TOK, TOK), 1)).astype(BF16)
-        rank = jnp.sum(dot(hot.astype(BF16), before) * hot, axis=0, keepdims=True).astype(jnp.int32)
-        row = iota((2 * TOK, TOK), 0)
-        main = jnp.logical_and(row == ids * TILE + rank, jnp.logical_and(rank < TILE, row < TOK))
-        last = jnp.logical_and((row - TOK) // TILE == ids, jnp.logical_and(rank == TILE, row >= TOK))
-        pick = jnp.logical_or(main, last).astype(BF16)
+    def pack():
         place = iota((TOK, 128), 0) % TILE
+        folded = [jnp.zeros((TOK, 128), F32) for d in range(X)]
+        for mb in range(2):
+            ids = ids_row[mb]
+            hot = (iota((8, TOK), 0) == ids).astype(F32)
+            before = (iota((TOK, TOK), 0) < iota((TOK, TOK), 1)).astype(BF16)
+            rank = jnp.sum(dot(hot.astype(BF16), before) * hot, axis=0, keepdims=True).astype(jnp.int32)
+            row = iota((2 * TOK, TOK), 0)
+            main = jnp.logical_and(row == ids * TILE + rank, jnp.logical_and(rank < TILE, row < TOK))
+            last = jnp.logical_and((row - TOK) // TILE == ids, jnp.logical_and(rank == TILE, row >= TOK))
+            pick = jnp.logical_or(main, last).astype(BF16)
+            for d in range(X):
+                picked = dot(pick, cot[mb, :, d * SLICE : (d + 1) * SLICE])
+                sent[mb][d, :, 0:SLICE] = picked[0:TOK].astype(BF16)
+                for k in range(CHUNKS):
+                    folded[d] = jnp.where(
+                        place == mb * 8 + k, picked[TOK:, k * 128 : (k + 1) * 128], folded[d]
+                    )
         for d in range(X):
-            picked = dot(pick, cot[mb, :, d * SLICE : (d + 1) * SLICE])
-            sent[mb, d, :, 0:SLICE] = picked[0:TOK].astype(BF16)
-            folded = jnp.zeros((TOK, 128), F32)
-            for k in range(CHUNKS):
-                folded = jnp.where(place == k, picked[TOK:, k * 128 : (k + 1) * 128], folded)
-            sent[mb, d, :, SLICE:WIDE] = folded.astype(BF16)
+            sent0[d, :, SLICE:WIDE] = folded[d].astype(BF16)
 
     def dispatch(mb):
         def one(step, carry):
@@ -112,8 +125,8 @@
             d = (x + 1 + step) % X
             near = jnp.where(z <= 2 * e, 2 * e, 2 * e + 1)
             target = near * X + d
-            src = sent.at[mb, d, rows16(e), :]
-            dst = routed.at[mb, rows16(me), :]
+            src = sent[mb].at[d, rows16(e), :]
+            dst = routed[mb].at[rows16(me), :]
 
             @pl.when(target == me)
             def _():
@@ -129,22 +142,22 @@
 
         lax.fori_loop(0, X * EXPERTS, one, 0)
 
-    def relay(mb, first, last):
+    def relay(mb):
         def one(step, carry):
             plane = z + away * step
-            block = routed.at[mb, band(plane), :]
+            block = routed[mb].at[band(plane), :]
             waited(block, routed_sem.at[mb, plane])
             pltpu.make_async_remote_copy(
                 block, block, relay_sem.at[mb, plane], routed_sem.at[mb, plane], **at(mate_id)
             ).start()
             return carry
 
-        lax.fori_loop(first, last, one, 0)
+        lax.fori_loop(0, owned, one, 0)
 
     def arrivals(mb):
         def one(step, carry):
             plane = mate - away * step
-            waited(routed.at[mb, band(plane), :], routed_sem.at[mb, plane])
+            waited(routed[mb].at[band(plane), :], routed_sem.at[mb, plane])
             return carry
 
         lax.fori_loop(0, others, one, 0)
@@ -173,13 +186,13 @@
 
     def first_product(mb):
         row = iota((CHUNKS * SOURCES, MAIN), 0)
-        unfold = (iota((CHUNKS * SOURCES, MAIN), 1) == (row % SOURCES) * TILE + row // SOURCES).astype(BF16)
-        tail = dot(unfold, routed[mb, :, SLICE:WIDE]).astype(BF16)
+        unfold = (iota((CHUNKS * SOURCES, MAIN), 1) == (row % SOURCES) * TILE + mb * 8 + row // SOURCES).astype(BF16)
+        tail = dot(unfold, routed0[:, SLICE:WIDE]).astype(BF16)
         tail = jnp.concatenate(
             [tail[k * SOURCES : (k + 1) * SOURCES] for k in range(CHUNKS)], axis=1
         )
         for j in range(X):
-            a_sent[mb, j, 0:MAIN] = dot_t(routed[mb, :, 0:SLICE], wd[j]).astype(BF16)
+            a_sent[mb, j, 0:MAIN] = dot_t(routed[mb][:, 0:SLICE], wd[j]).astype(BF16)
             a_sent[mb, j, MAIN:ROWS] = dot_t(tail, wd[j]).astype(BF16)
         for j in range(1, X):
             pltpu.make_async_remote_copy(
@@ -230,18 +243,16 @@
             folded = jnp.where(place == k, spread[:, k * 128 : (k + 1) * 128], folded)
         part[mb, :, SLICE:WIDE] = folded.astype(BF16)
 
-        def one(step, carry):
-            plane = mate - away * step
+    def send_back(mb, stage):
+        def give(step, carry):
+            plane = mate - away * (others - 1 - step)
             pltpu.make_async_remote_copy(
                 part.at[mb, band(plane), :], mate_part.at[mb, band(plane), :],
                 mate_send.at[mb, plane], mate_sem.at[mb, plane], **at(mate_id),
             ).start()
             return carry
 
-        lax.fori_loop(0, others, one, 0)
-
-    def send_back(mb):
-        def one(step, carry):
+        def take(step, carry):
             plane = z + away * (owned - 1 - step)
             rows = band(plane)
             waited(mate_part.at[mb, rows, :], mate_sem.at[mb, plane])
@@ -268,7 +279,10 @@
             lax.fori_loop(0, X, to, 0)
             return carry
 
-        lax.fori_loop(0, owned, one, 0)
+        if stage == 0:
+            lax.fori_loop(0, others, give, 0)
+        else:
+            lax.fori_loop(0, owned, take, 0)
 
     def finish(mb):
         waited(back.at[mb], back_sem.at[mb])
@@ -301,29 +315,31 @@
                 out[mb, :, across] = dx
         scores[mb] = jnp.sum(jnp.where(lane == rank, score, 0.0), axis=1, keepdims=True)
 
-    pack(0)
+    loads[0].wait()
+    pack()
     pl.semaphore_wait(barrier, X * Z - 1 + ends)
     dispatch(0)
     weights()
-    pack(1)
+    relay(0)
     dispatch(1)
-    relay(0, 0, owned)
     arrivals(0)
     weights_here(0, wd)
     first_product(0)
-    half = (owned + 1) // 2
-    relay(1, 0, half)
+    relay(1)
+    loads[1].wait()
+    loads[2].wait()
     activate(0)
-    relay(1, half, owned)
-    arrivals(1)
-    first_product(1)
     weights_here(1, wg)
     weights_here(2, wu)
     second_product(0)
+    send_back(0, 0)
+    arrivals(1)
+    first_product(1)
     activate(1)
-    send_back(0)
+    send_back(0, 1)
     second_product(1)
-    send_back(1)
+    send_back(1, 0)
+    send_back(1, 1)
     finish(0)
 
     @pl.when(sec > 0)
@@ -339,11 +355,11 @@
     finish(1)
 
     for mb in range(2):
-        waited(routed.at[mb, pl.ds(0, (X * EXPERTS - 1) * TILE), :], send_sem.at[mb])
+        waited(routed[mb].at[pl.ds(0, (X * EXPERTS - 1) * TILE), :], send_sem.at[mb])
 
         def relayed(step, carry):
             plane = z + away * step
-            waited(routed.at[mb, band(plane), :], relay_sem.at[mb, plane])
+            waited(routed[mb].at[band(plane), :], relay_sem.at[mb, plane])
             rows = total.at[mb, band(plane), :]
 
             @pl.when(plane == z)
@@ -386,7 +402,7 @@
         return jnp.concatenate([main, saved[0, :, :, TILE, :]], axis=1)
 
     vmem = pl.BlockSpec(memory_space=pltpu.VMEM)
-    hbm = pl.BlockSpec(memory_space=pl.ANY)
+    hbm = pl.BlockSpec(memory_space=pltpu.HBM)
     dma = pltpu.SemaphoreType.DMA
     grads, scores = pl.pallas_call(
         kernel,
@@ -394,11 +410,17 @@
             jax.ShapeDtypeStruct((2, TOK, D), BF16),
             jax.ShapeDtypeStruct((2, TOK, 1), F32),
         ),
-        in_specs=[vmem] * 6 + [hbm] * 3,
+        in_specs=[vmem] * 3 + [hbm] * 6,
         out_specs=(vmem, vmem),
         scratch_shapes=[
-            pltpu.VMEM((2, X, TOK, WIDE), BF16),
-            pltpu.VMEM((2, MAIN, WIDE), BF16),
+            pltpu.VMEM((2, TOK, D), BF16),
+            pltpu.VMEM((2, ROWS, FH), BF16),
+            pltpu.VMEM((2, ROWS, FH), BF16),
+            dma((3,)),
+            pltpu.VMEM((X, TOK, WIDE), BF16),
+            pltpu.VMEM((X, TOK, SLICE), BF16),
+            pltpu.VMEM((MAIN, WIDE), BF16),
+            pltpu.VMEM((MAIN, SLICE), BF16),
             pltpu.VMEM((X, FH, SLICE), BF16),
             pltpu.VMEM((X, SLICE, FH), BF16),
             pltpu.VMEM((X, SLICE, FH), BF16),
@@ -428,7 +450,7 @@
             dma,
         ],
         compiler_params=pltpu.CompilerParams(
-            collective_id=0, has_side_effects=True, vmem_limit_bytes=48 * 1024 * 1024
+            collective_id=0, has_side_effects=True, vmem_limit_bytes=VMEM_MB * 1024 * 1024
         ),
         cost_estimate=pl.CostEstimate(
             flops=6 * 2 * ROWS * D * FH, bytes_accessed=8 * 1024 * 1024, transcendentals=2 * ROWS * FH

time: 199 us -> 188 us (0.945)
  the two profiles are of different devices: /device:TPU:112 before, /device:TPU:40 now
where the time goes in v2:
time: 188 us; the launch traced here: 187 us
  Pallas kernels  178 us (95%)
  local copies, waits for them, and re-layouts  7.37 us (4%)
    pallas_call x1, Pallas kernels, on_device(): pl.pallas_call(kernel, out_shape=(jax.ShapeDtypeStruct((2, TOK, D), BF16)...  178 us
    unnamed x13, local copies, waits for them, and re-layouts  3.77 us

profile of v2, /device:TPU:40, one launch (start us, length us, event | category | flops | bytes accessed | tf_op | source)
XLA Modules:
  0.0 187.2 jit_solution(17248451068369836480)
XLA Ops:
  0.6 0.7 slice_bitcast_fusion.1
  1.4 0.0 copy-start.5
  1.4 0.7 slice_bitcast_fusion
  2.1 0.0 copy-done.5
  2.1 0.0 copy-start
  2.1 0.1 copy.24.prob
  2.2 0.6 copy-done
  2.8 0.0 slice-start
  2.8 0.1 copy.22.ids_col
  2.9 0.0 copy-start.3
  2.9 0.8 slice-done
  3.7 0.0 slice-start.1
  3.7 0.1 copy.18
  3.8 0.0 copy-start.2
  3.8 0.9 slice-done.1
  4.7 0.0 copy-start.1
  4.7 0.1 copy.20
  4.9 0.0 copy-done.3
  4.9 0.2 copy-done.2
  5.1 0.9 copy-done.1
  6.0 0.0 copy-start.4
  6.0 1.2 copy-done.4
  7.2 178.4 %shard_map.95 = (bf16[2,64,3584]{2,1,0:T(8,128)(2,1)S(1)}, f32[2,64,1]{2,1,0:T(8,128)S(1)}) custom-call(s32[2,64,1]{2,1,0:T(8,128)S(1)} %copy.22.ids_col, s32[2,1,64]{2,1,0:T(1,128)S(1)} %bitcast.25, f32[2,64,1]{2,1,0:T(8,128)S(1)} %copy.24.prob, bf16[2,64,3584]{2,1,0:T(8,128)(2,1)S(1)} %bitcast.26, bf16[2,544,128]{2,1,0:T(8,128)(2,1)S(1)} %get-tuple-element.10.gate_hbm, ...), custom_call_target="tpu_custom_call" | custom-call | flops 2994733056 | bytes 8388608 | tf_op jit(solution)/shard_map/pallas_call | solution.py:407
  185.6 0.7 reduce
  186.3 0.9 copy.29
  (1 shorter events, 0.0 us)
Async XLA Ops:
  1.4 0.7 copy-start.5
  2.1 0.7 copy-start
  2.8 0.9 slice-start
  2.9 2.0 %copy-start.3 = (bf16[1,3584,128]{2,1,0:T(8,128)(2,1)S(1)}, bf16[1,3584,128]{2,1,0:T(8,128)(2,1)}, u32[]{:S(2)}) copy-start(bf16[1,3584,128]{2,1,0:T(8,128)(2,1)} %param.14) | copy-start | bytes 2752516
  3.7 1.0 slice-start.1
  3.8 1.3 copy-start.2
  4.7 1.2 copy-start.1
  6.0 1.2 copy-start.4

commit v3 on v2

--- a/solution.py
+++ b/solution.py
@@ -44,7 +44,7 @@
 
 
 def kernel(
-    ids_col, ids_row, prob, cot_hbm, gate_hbm, up_hbm, w_gate, w_up, w_down,
+    ids_row, prob, cot_hbm, gate_hbm, up_hbm, w_gate, w_up, w_down,
     out, scores,
     cot, saved_gate, saved_up, in_sem,
     sent0, sent1, routed0, routed1, wd, wg, wu, a_sent, a_got, hidden, part, mate_part, total, back, handed,
@@ -118,11 +118,10 @@
         for d in range(X):
             sent0[d, :, SLICE:WIDE] = folded[d].astype(BF16)
 
-    def dispatch(mb):
+    def dispatch(mb, turn):
         def one(step, carry):
-            far = step // X
-            e = jnp.where(z < Z // 2, EXPERTS - 1 - far, far)
-            d = (x + 1 + step) % X
+            e = jnp.where(z < Z // 2, EXPERTS - 1 - step, step)
+            d = (x + 1 + turn) % X
             near = jnp.where(z <= 2 * e, 2 * e, 2 * e + 1)
             target = near * X + d
             src = sent[mb].at[d, rows16(e), :]
@@ -130,25 +129,25 @@
 
             @pl.when(target == me)
             def _():
-                pltpu.make_async_copy(src, dst, routed_sem.at[mb, z]).start()
+                pltpu.make_async_copy(src, dst, routed_sem.at[mb, me]).start()
 
             @pl.when(target != me)
             def _():
                 pltpu.make_async_remote_copy(
-                    src, dst, send_sem.at[mb], routed_sem.at[mb, z], **at(target)
+                    src, dst, send_sem.at[mb], routed_sem.at[mb, me], **at(target)
                 ).start()
 
             return carry
 
-        lax.fori_loop(0, X * EXPERTS, one, 0)
-
-    def relay(mb):
+        lax.fori_loop(0, EXPERTS, one, 0)
+
+    def relay(mb, turn):
         def one(step, carry):
-            plane = z + away * step
-            block = routed[mb].at[band(plane), :]
-            waited(block, routed_sem.at[mb, plane])
+            source = (z + away * step) * X + (x + X - 1 - turn) % X
+            block = routed[mb].at[rows16(source), :]
+            waited(block, routed_sem.at[mb, source])
             pltpu.make_async_remote_copy(
-                block, block, relay_sem.at[mb, plane], routed_sem.at[mb, plane], **at(mate_id)
+                block, block, relay_sem.at[mb, source], routed_sem.at[mb, source], **at(mate_id)
             ).start()
             return carry
 
@@ -156,13 +155,13 @@
 
     def arrivals(mb):
         def one(step, carry):
-            plane = mate - away * step
-            waited(routed[mb].at[band(plane), :], routed_sem.at[mb, plane])
-            return carry
-
-        lax.fori_loop(0, others, one, 0)
-
-    def weights():
+            source = (mate - away * (step // X)) * X + step % X
+            waited(routed[mb].at[rows16(source), :], routed_sem.at[mb, source])
+            return carry
+
+        lax.fori_loop(0, X * others, one, 0)
+
+    def weights(wanted):
         for j in range(X):
             d = (x + j) % X
             across = pl.ds(pl.multiple_of(d * SLICE, 128), SLICE)
@@ -172,6 +171,8 @@
                 (w_up.at[across, :], wu.at[j]),
             )
             for which, (src, dst) in enumerate(pairs):
+                if which not in wanted:
+                    continue
                 if j == 0:
                     pltpu.make_async_copy(src, dst, w_own.at[which]).start()
                 else:
@@ -286,7 +287,12 @@
 
     def finish(mb):
         waited(back.at[mb], back_sem.at[mb])
-        ids = ids_col[mb]
+        same = iota((TOK, TOK), 0) == iota((TOK, TOK), 1)
+
+        def upright(row):
+            return jnp.sum(jnp.where(same, row, 0.0), axis=1, keepdims=True)
+
+        ids = upright(ids_row[mb].astype(F32)).astype(jnp.int32)
         lane = iota((TOK, 128), 1)
         hot = (lane == ids).astype(F32)
         before = (iota((TOK, TOK), 1) < iota((TOK, TOK), 0)).astype(BF16)
@@ -299,7 +305,7 @@
         group.append((column == ids * TILE + SCORE_ROW).astype(F32))
         pick = jnp.concatenate(group, axis=0).astype(BF16)
         score = jnp.zeros((TOK, 128), F32)
-        weight = prob[mb]
+        weight = upright(prob[mb])
         for d in range(X):
             tail = dot(pick, back[mb, d, :, SLICE:WIDE])
             score = score + tail[CHUNKS * TOK :]
@@ -313,19 +319,25 @@
                 handed[:, across] = dx
             else:
                 out[mb, :, across] = dx
-        scores[mb] = jnp.sum(jnp.where(lane == rank, score, 0.0), axis=1, keepdims=True)
+        score = jnp.sum(jnp.where(lane == rank, score, 0.0), axis=1, keepdims=True)
+        scores[mb] = jnp.sum(jnp.where(same, score, 0.0), axis=0, keepdims=True)
 
     loads[0].wait()
     pack()
     pl.semaphore_wait(barrier, X * Z - 1 + ends)
-    dispatch(0)
-    weights()
-    relay(0)
-    dispatch(1)
+    for turn in range(X):
+        dispatch(0, turn)
+    weights((0,))
+    weights((1, 2))
+    for turn in range(X):
+        relay(0, turn)
+    for turn in range(X):
+        dispatch(1, turn)
     arrivals(0)
     weights_here(0, wd)
     first_product(0)
-    relay(1)
+    for turn in range(X):
+        relay(1, turn)
     loads[1].wait()
     loads[2].wait()
     activate(0)
@@ -359,7 +371,9 @@
 
         def relayed(step, carry):
             plane = z + away * step
-            waited(routed[mb].at[band(plane), :], relay_sem.at[mb, plane])
+            for other in range(X):
+                source = plane * X + other
+                waited(routed[mb].at[rows16(source), :], relay_sem.at[mb, source])
             rows = total.at[mb, band(plane), :]
 
             @pl.when(plane == z)
@@ -408,9 +422,9 @@
         kernel,
         out_shape=(
             jax.ShapeDtypeStruct((2, TOK, D), BF16),
-            jax.ShapeDtypeStruct((2, TOK, 1), F32),
+            jax.ShapeDtypeStruct((2, 1, TOK), F32),
         ),
-        in_specs=[vmem] * 3 + [hbm] * 6,
+        in_specs=[vmem] * 2 + [hbm] * 6,
         out_specs=(vmem, vmem),
         scratch_shapes=[
             pltpu.VMEM((2, TOK, D), BF16),
@@ -433,8 +447,8 @@
             pltpu.VMEM((2, X, TOK, WIDE), BF16),
             pltpu.VMEM((TOK, D), BF16),
             dma((2,)),
-            dma((2, Z)),
-            dma((2, Z)),
+            dma((2, SOURCES)),
+            dma((2, SOURCES)),
             dma((3, X - 1)),
             dma((3, X - 1)),
             dma((3,)),
@@ -456,9 +470,8 @@
             flops=6 * 2 * ROWS * D * FH, bytes_accessed=8 * 1024 * 1024, transcendentals=2 * ROWS * FH
         ),
     )(
-        routes[0],
         routes[0].reshape(2, 1, TOK),
-        gate_prob[0],
+        gate_prob[0].reshape(2, 1, TOK),
         cotangent[0],
         by_row(saved_gate),
         by_row(saved_up),
@@ -466,7 +479,7 @@
         w_up[0],
         w_down[0],
     )
-    return grads[None], scores[None]
+    return grads[None], scores.reshape(1, 2, TOK, 1)
 
 
 def solution(mesh):

time: 188 us -> 179 us (0.952)
  the two profiles are of different devices: /device:TPU:40 before, /device:TPU:112 now
where the time goes in v3:
time: 179 us
  Pallas kernels  172 us (96%)
  local copies, waits for them, and re-layouts  5.96 us (3%)
    pallas_call x1, Pallas kernels, on_device(): pl.pallas_call(kernel, out_shape=(jax.ShapeDtypeStruct((2, TOK, D), BF16)...  172 us
    unnamed x14, local copies, waits for them, and re-layouts  4 us

profile of v3, /device:TPU:112, one launch (start us, length us, event | category | flops | bytes accessed | tf_op | source)
XLA Modules:
  0.0 179.0 jit_solution(8316517165432255585)
XLA Ops:
  0.6 0.0 slice-start.1
  0.6 0.8 slice_bitcast_fusion.1
  1.4 0.0 slice-start
  1.4 0.8 slice_bitcast_fusion
  2.2 0.0 copy-start.2
  2.2 0.2 slice-done
  2.4 0.1 copy.10
  2.5 0.0 copy-start.1
  2.5 0.0 slice-done.1
  2.5 0.0 copy-start
  2.5 0.1 copy.12
  2.6 0.0 copy-start.5
  2.7 0.0 copy-start.4
  2.7 0.7 copy-done.2
  3.4 0.4 copy-done.1
  3.8 0.3 copy-done
  4.0 0.0 copy-done.5
  4.0 0.0 copy-done.4
  4.0 0.0 copy-start.3
  4.0 1.2 copy-done.3
  5.2 172.3 %shard_map.95 = (bf16[2,64,3584]{2,1,0:T(8,128)(2,1)S(1)}, f32[2,1,64]{2,1,0:T(1,128)S(1)}) custom-call(s32[2,1,64]{2,1,0:T(1,128)S(1)} %bitcast.30, f32[2,1,64]{2,1,0:T(1,128)S(1)} %bitcast.31, bf16[2,64,3584]{2,1,0:T(8,128)(2,1)S(1)} %bitcast.26, bf16[2,544,128]{2,1,0:T(8,128)(2,1)S(1)} %get-tuple-element.8.gate_hbm, ...), custom_call_target="tpu_custom_call" | custom-call | flops 2994733056 | bytes 8388608 | tf_op jit(solution)/shard_map/pallas_call | solution.py:421
  177.5 0.9 copy.21
  178.4 0.6 copy.22
  (1 shorter events, 0.0 us)
Async XLA Ops:
  0.6 1.9 %slice-start.1 = ((bf16[1,2,32,17,128]{4,2,3,1,0:T(8,128)(2,1)}), bf16[1,2,32,16,128]{4,2,3,1,0:T(8,128)(2,1)S(1)}, s32[]{:S(2)}) async-start(bf16[1,2,32,17,128]{4,2,3,1,0:T(8,128)(2,1)} %param.12), calls=%async_computation.1 | async-start | bytes 524288 | tf_op jit(solution)/shard_map/slice | solution.py:415
  1.4 1.0 slice-start
  2.2 1.2 copy-start.2
  2.5 1.3 copy-start.1
  2.5 1.5 copy-start
  2.6 1.4 copy-start.5
  2.7 1.3 copy-start.4
  4.0 1.2 copy-start.3
